TPU v7x, 256 devices: a whole 4x4x8 slice. The times are simulated.
256 devices in a mesh: blk: 16 (over z_hi, y, core), tp: 16 (over z_lo, x).
Axes of the slice: x: 4, y: 4, z: 8 (z_hi: 2, z_lo: 4; z = z_hi * 4 + z_lo), core: 2. Of those that a mesh axis runs over, the one named last changes fastest.
Arguments:
- hidden_in: bfloat16 [8192, 4096], P('blk', 'tp'), may hold values from -16 to 16
- w_query: bfloat16 [4096, 4096], P(None, 'tp'), may hold values from -0.09375 to 0.09375
- w_keyval: bfloat16 [4096, 2048], P('tp'), may hold values from -0.09375 to 0.09375
- routing: int32 [16, 1], replicated, may hold values from 0 to 3; in each aligned block of 16 rows (0 to 15, 16 to 31, ...) at most 8 rows name the same one
- hosts: int32 [16], replicated, may hold values from 0 to 15, each once
Outputs:
- attended: bfloat16 [8192, 4096], P('blk', 'tp')
- decode_cache: bfloat16 [16, 8, 512, 2048], P('blk', None, None, 'tp')
Inputs may be any that keep to these rules, and one draw needn't show every extreme that they name: `routing`: each prompt block names one decode instance; each of the 4 instances is named by at least one block and by at most 8, a bound that some instance reaches. `hosts`: A permutation of the 16 instance ids; only the first 4 entries are used.
All inputs are finite; a program needn't handle non-finite values.
Results may differ from a plain program's by a relative error of at most 0.007.
The roundings to bfloat16 on the way count: a program that leaves them out, or rounds other values in their place, can miss the bound.
Values may be sent and summed in bfloat16 or wider, within the bound.
A program may use at most 128 MiB of HBM per device.

v0:
```python
import jax
import jax.numpy as jnp
from jax import lax
from jax.sharding import PartitionSpec as P

HEADS = 32
KVH = 8
HD = 128
DECODE = 4


def spread_heads(columns, tp_count, heads_dev, group_size, needed_width):
    pieces = []
    for device in range(tp_count):
        start = device * heads_dev // group_size * 2 * HD
        pieces.append(columns[:, start : start + needed_width])
    return jnp.concatenate(pieces, axis=1)


def local(hidden_in, w_query, w_keyval, routing, hosts):
    tok_rows = hidden_in.shape[0]
    tp_count = lax.axis_size("tp")
    blk_count = lax.axis_size("blk")
    tp_index = lax.axis_index("tp")
    blk_index = lax.axis_index("blk")
    heads_dev = w_query.shape[1] // HD
    group_size = HEADS // KVH
    kv_local = max(1, heads_dev // group_size)
    q_per = heads_dev // kv_local
    shard_width = w_keyval.shape[1] // tp_count
    needed_width = kv_local * 2 * HD
    capacity = blk_count // 2
    queries_flat = jnp.dot(
        lax.all_gather(hidden_in, "tp", axis=1, tiled=True),
        w_query,
        preferred_element_type=jnp.float32,
    ).astype(jnp.bfloat16)
    kv_first = tp_index * heads_dev // group_size
    partial_kv = jnp.dot(hidden_in, w_keyval, preferred_element_type=jnp.float32)
    spread_kv = spread_heads(partial_kv, tp_count, heads_dev, group_size, needed_width)
    local_kv = lax.psum_scatter(spread_kv, "tp", scatter_dimension=1, tiled=True).astype(
        jnp.bfloat16
    )
    column_start = tp_index * shard_width - kv_first * 2 * HD
    own_kv = lax.dynamic_slice_in_dim(local_kv, column_start, shard_width, 1)
    assigned = routing[:, 0]
    block_ids = jnp.arange(blk_count, dtype=jnp.int32)
    earlier = (assigned[:, None] == assigned[None, :]) & (block_ids[None, :] < block_ids[:, None])
    slot_of = jnp.sum(earlier.astype(jnp.int32), axis=1)
    decode_ids = jnp.arange(DECODE, dtype=jnp.int32)
    owners = jnp.sum(
        (assigned[:, None] == decode_ids[None, :]).astype(jnp.int32) * hosts[None, :DECODE], axis=1
    )
    hosted = owners == blk_index
    queries = queries_flat.reshape(tok_rows, kv_local, q_per, HD)
    positions = blk_index * tok_rows + jnp.arange(tok_rows, dtype=jnp.int32)
    score_scale = HD ** (-0.5)
    cache_init = jnp.zeros((1, shard_width), jnp.bfloat16)
    shard_part = lax.all_gather(local_kv, "blk", axis=0, tiled=True)
    row_count = shard_part.shape[0]
    kv_pairs = shard_part.reshape(row_count, kv_local, 2, HD)
    key_rows = kv_pairs[:, :, 0]
    value_rows = kv_pairs[:, :, 1]
    scores = (
        jnp.einsum("tkgd,nkd->kgtn", queries, key_rows, preferred_element_type=jnp.float32)
        * score_scale
    )
    allowed = jnp.arange(row_count, dtype=jnp.int32)[None, :] <= positions[:, None]
    largest = jnp.full((kv_local, q_per, tok_rows), -1e30, jnp.float32)
    new_largest = jnp.maximum(largest, jnp.max(jnp.where(allowed, scores, -1e30), axis=-1))
    weights = jnp.where(allowed, jnp.exp(scores - new_largest[..., None]), 0.0)
    denominator = jnp.sum(weights, axis=-1)
    update = jnp.einsum(
        "kgtn,nkd->kgtd",
        weights.astype(jnp.bfloat16),
        value_rows,
        preferred_element_type=jnp.float32,
    )
    numerator = update
    softmax_state = (new_largest, denominator, numerator)
    cache_rows = cache_init
    final_state, cache_rows = (softmax_state, cache_rows)
    largest, denominator, numerator = final_state
    heads_out = numerator / denominator[..., None]
    attended = (
        jnp.transpose(heads_out, (2, 0, 1, 3))
        .reshape(tok_rows, heads_dev * HD)
        .astype(jnp.bfloat16)
    )
    gathered = lax.all_gather(own_kv, "blk", axis=0, tiled=True).reshape(
        blk_count, tok_rows, shard_width
    )
    slot_ids = jnp.arange(capacity, dtype=jnp.int32)
    select = ((slot_of[None, :] == slot_ids[:, None]) & hosted[None, :]).astype(jnp.bfloat16)
    decode_cache = jnp.einsum(
        "sb,btw->stw", select, gathered, preferred_element_type=jnp.float32
    ).astype(jnp.bfloat16)[None]
    return (attended, decode_cache)


def solution(mesh):
    in_specs = (P("blk", "tp"), P(None, "tp"), P("tp", None), P(), P())
    out_specs = (P("blk", "tp"), P("blk", None, None, "tp"))
    return jax.shard_map(local, mesh=mesh, in_specs=in_specs, out_specs=out_specs, check_vma=False)
```

profile of v0, /device:TPU:1, one launch (start us, length us, event | category | flops | bytes accessed | tf_op | source)
XLA Modules:
  0.0 442.2 jit_solution(9640649593018121349)
XLA Ops:
  7.2 0.0 copy-start
  7.2 0.0 reduce-scatter.2.cloned.1.call-start
  7.2 2.2 fusion.38
  9.4 0.8 slice_dynamic-update-slice_fusion.8
  10.2 1.1 slice_dynamic-update-slice_fusion.6
  11.4 1.0 slice_dynamic-update-slice_fusion.5
  12.4 1.2 slice_dynamic-update-slice_fusion.4
  13.6 1.1 slice_dynamic-update-slice_fusion.3
  14.7 0.0 copy-start.3
  14.7 0.0 copy-start.4
  14.7 1.2 slice_dynamic-update-slice_fusion.2
  15.9 1.1 slice_dynamic-update-slice_fusion.1
  17.0 1.1 slice_dynamic-update-slice_fusion
  18.1 0.8 slice_dynamic-update-slice_fusion.7
  18.9 0.0 reduce-scatter.2.cloned.1.call-update
  18.9 0.0 all-gather.6.cloned.1.call-start
  19.0 0.7 all-gather.6.cloned.1.call-update
  19.7 0.0 all-gather.8.cloned.1.call-start
  19.8 102.5 %reduce-scatter.2.cloned.1.call-done = f32[512,256]{1,0:T(8,128)} async-done(((f32[512,4096]{1,0:T(8,128)}), f32[512,256]{1,0:T(8,128)}) %reduce-scatter.2.cloned.1.call-update) | async-done | bytes 524304 | tf_op jit(solution)/shard_map/reduce_scatter | solution.py:41
  122.2 1.1 convert_element_type.29
  123.3 0.0 copy-start.2
  123.3 0.7 constant_dynamic-slice_fusion
  124.0 0.0 all-gather.8.cloned.1.call-update
  124.1 0.0 all-gather.4.cloned.1.call-start
  124.1 0.0 copy-done.2
  124.1 0.5 all-gather.4.cloned.1.call-update
  124.7 0.0 copy-done.3
  124.7 0.2 convert_reduce_fusion
  124.9 0.0 copy-done.4
  124.9 0.1 select_reduce_fusion
  125.0 5.5 %iota_compare_fusion = pred[512,8192]{0,1:T(8,128)(4,1)} fusion(s32[512]{0:T(512)S(1)} %iota_add_fusion), kind=kLoop, calls=%fused_computation.8 | loop fusion | flops 4194304 | bytes 4196352 | tf_op jit(solution)/shard_map/le | solution.py:68
  130.5 78.2 %all-gather.6.cloned.1.call-done = bf16[512,4096]{1,0:T(8,128)(2,1)} async-done(((bf16[512,256]{1,0:T(8,128)(2,1)}), bf16[512,4096]{1,0:T(8,128)(2,1)}) %all-gather.6.cloned.1.call-update) | async-done | bytes 4194320 | tf_op jit(solution)/shard_map/all_gather | solution.py:34
  208.7 0.0 copy-done
  208.7 3.5 convolution_convert_fusion
  212.2 73.4 %all-gather.8.cloned.1.call-done = bf16[8192,128]{1,0:T(8,128)(2,1)} async-done(((bf16[512,128]{1,0:T(8,128)(2,1)}), bf16[8192,128]{1,0:T(8,128)(2,1)}) %all-gather.8.cloned.1.call-update) | async-done | bytes 2097168 | tf_op jit(solution)/shard_map/all_gather | solution.py:90
  285.6 2.8 fusion.16
  288.5 1.1 copy.20
  289.6 72.1 %all-gather.4.cloned.1.call-done = bf16[8192,256]{1,0:T(8,128)(2,1)} async-done(((bf16[512,256]{1,0:T(8,128)(2,1)}), bf16[8192,256]{1,0:T(8,128)(2,1)}) %all-gather.4.cloned.1.call-update) | async-done | bytes 4194320 | tf_op jit(solution)/shard_map/all_gather | solution.py:59
  361.7 6.9 %reshape.58 = bf16[8192,1,2,128]{3,2,0,1:T(2,128)(2,1)} reshape(bf16[8192,256]{1,0:T(8,128)(2,1)} %all-gather.4.cloned.1.call-done) | data formatting | bytes 8388608 | tf_op jit(solution)/shard_map/reshape | solution.py:61
  368.7 9.7 %fusion.37 = (bf16[8192,1,1,128]{3,2,0,1:T(2,128)(2,1)}, bf16[8192,1,1,128]{3,2,0,1:T(2,128)(2,1)}) fusion(bf16[8192,1,2,128]{3,2,0,1:T(2,128)(2,1)} %reshape.58), kind=kLoop, calls=%fused_computation.46 | loop fusion | bytes 8388608 | tf_op jit(solution)/shard_map/slice | solution.py:63
  378.4 9.2 %copy.23 = bf16[8192,1,1,128]{0,3,2,1:T(8,128)(2,1)} copy(bf16[8192,1,1,128]{3,2,0,1:T(2,128)(2,1)} %get-tuple-element.6) | data formatting | bytes 4194304
  387.6 16.2 %fusion = (f32[2,512]{1,0:T(2,128)S(1)}, f32[8192,512,2]{1,0,2:T(8,128)}) fusion(pred[512,8192]{0,1:T(8,128)(4,1)} %iota_compare_fusion, bf16[512,2,128]{0,2,1:T(8,128)(2,1)S(1)} %bitcast.69, bf16[8192,1,1,128]{3,2,0,1:T(2,128)(2,1)} %get-tuple-element.7), kind=kOutput, calls=%fused_computation.2 | convolution fusion | flops 2172648448 | bytes 40112128 | tf_op jit(solution)/shard_map/tkgd,nkd->kgtn/dot_general | solution.py:65
  403.8 15.1 %fusion.3 = f32[2,512]{1,0:T(2,128)S(1)} fusion(f32[8192,512,2]{1,0,2:T(8,128)} %get-tuple-element.9, f32[2,512]{1,0:T(2,128)S(1)} %broadcast_maximum_fusion, pred[512,8192]{0,1:T(8,128)(4,1)} %iota_compare_fusion), kind=kLoop, calls=%fused_computation.5 | loop fusion | flops 33553408 | bytes 37756928 | tf_op jit(solution)/shard_map/reduce_sum | solution.py:72
  418.9 0.0 copy-start.1
  418.9 15.9 %fusion.24 = bf16[2,512,128]{1,2,0:T(8,128)(2,1)S(1)} fusion(f32[8192,512,2]{1,0,2:T(8,128)} %get-tuple-element.9, f32[2,512]{1,0:T(2,128)S(1)} %broadcast_maximum_fusion, pred[512,8192]{0,1:T(8,128)(4,1)} %iota_compare_fusion, bf16[8192,1,1,128]{0,3,2,1:T(8,128)(2,1)} %copy.23, f32[2,512]{1,0:T(2,128)S(1)} %fusion.3), kind=kOutput, calls=%fused_computation.27 | convolution fusion | flops 2181300224 | bytes 40116224 | tf_op jit(solution)/shard_map/kgtn,nkd->kgtd/dot_general | solution.py:73
  434.8 0.8 copy.19
  435.6 0.0 copy-done.1
  (3 shorter events, 0.0 us)
Async XLA Ops:
  7.2 201.5 %copy-start = (bf16[4096,256]{1,0:T(8,128)(2,1)S(1)}, bf16[4096,256]{1,0:T(8,128)(2,1)}, u32[]{:S(2)}) copy-start(bf16[4096,256]{1,0:T(8,128)(2,1)} %param.6) | copy-start | bytes 6291460
  7.2 115.0 %reduce-scatter.2.cloned.1.call-start = ((), (), s32[]{:S(2)}) async-start(), calls=%async_computation.1 | async-start | bytes 8912896 | tf_op jit(solution)/shard_map/reduce_scatter | solution.py:41
  14.7 110.0 %copy-start.3 = (s32[16,1]{0,1:T(1,128)S(1)}, s32[16,1]{0,1:T(1,128)}, u32[]{:S(2)}) copy-start(s32[16,1]{0,1:T(1,128)} %param.8) | copy-start | bytes 196
  14.7 110.2 %copy-start.4 = (s32[16]{0:T(128)S(1)}, s32[16]{0:T(128)}, u32[]{:S(2)}) copy-start(s32[16]{0:T(128)} %param.9) | copy-start | bytes 196
  18.9 189.7 %all-gather.6.cloned.1.call-start = ((), (), s32[]{:S(2)}) async-start(), calls=%async_computation.3 | async-start | bytes 4456448 | tf_op jit(solution)/shard_map/all_gather | solution.py:34
  19.7 265.9 %all-gather.8.cloned.1.call-start = ((), (), s32[]{:S(2)}) async-start(), calls=%async_computation.4 | async-start | bytes 2228224 | tf_op jit(solution)/shard_map/all_gather | solution.py:90
  123.3 0.8 copy-start.2
  124.1 237.6 %all-gather.4.cloned.1.call-start = ((), (), s32[]{:S(2)}) async-start(), calls=%async_computation.2 | async-start | bytes 4456448 | tf_op jit(solution)/shard_map/all_gather | solution.py:59
  418.9 16.7 %copy-start.1 = (bf16[4096,256]{1,0:T(8,128)(2,1)S(1)}, bf16[4096,256]{1,0:T(8,128)(2,1)}, u32[]{:S(2)}) copy-start(bf16[4096,256]{1,0:T(8,128)(2,1)} %param.6) | copy-start | bytes 6291460
Sparse Core Ops, SparseCore 0:
  19.1 103.1 reduce-scatter.1
  123.9 84.7 all-gather.5
  212.0 73.5 all-gather.7
  288.8 72.8 all-gather.3
where the time goes:
time: 443 us; the launch traced here: 442 us
  waiting for transfers between devices  327 us (74%)
  matrix products  40.6 us (9%)
  local copies, waits for them, and re-layouts  38.1 us (9%)
  other arithmetic  22 us (5%)
  between operations  13.9 us (3%)
    reduce_scatter x1, waiting for transfers between devices, local(): lax.psum_scatter(spread_kv, 'tp', scatter_dimension=1, tiled=True)  102 us
    all_gather x1, waiting for transfers between devices, local(): lax.all_gather(hidden_in, 'tp', axis=1, tiled=True)  78.2 us
    all_gather x1, waiting for transfers between devices, local(): lax.all_gather(own_kv, 'blk', axis=0, tiled=True)  73.4 us
    all_gather x1, waiting for transfers between devices, local(): shard_part = lax.all_gather(local_kv, 'blk', axis=0, tiled=True)  72.1 us
    unnamed x21, local copies, waits for them, and re-layouts  19.9 us
    dot_general x1, matrix products, local(): jnp.einsum('tkgd,nkd->kgtn', queries, key_rows, preferred_element_type=jn...  16.2 us
    dot_general x1, matrix products, local(): jnp.einsum('kgtn,nkd->kgtd', weights.astype(jnp.bfloat16), value_rows, pr...  15.9 us
    reduce_sum x1, other arithmetic, local(): denominator = jnp.sum(weights, axis=-1)  15.1 us
  transfers between devices with their start and end apart: 4, of which 4 were waited for; matrix products, arithmetic and copies ran while one was open for 3% of the time, Pallas kernels for 0%

commit v1 on v0

v1 whole, which is shorter than its diff:
```python
import functools

import jax
import jax.numpy as jnp
from jax import lax
from jax.experimental import pallas as pl
from jax.experimental.pallas import tpu as pltpu
from jax.sharding import PartitionSpec as P

HEADS = 32
KVH = 8
HD = 128
TOK = 512
CAP = 8
NB = 16
NT = 16
FD = 256
PART = 32
R = 2
RC = TOK // R
HC = RC // 2
TQ = 256
MESH = pl.DeviceIdType.MESH
LOG2E = 1.4426950408889634
SCALE2 = HD**-0.5 * LOG2E
NEG = -1e30


def kernel(
    hidden_ref, wq_ref, wkv_ref, routing_ref, hosts_ref,
    att_ref, cache_ref,
    hid, wq, wkv, kv, tmp, acc, qbuf, sbuf, cbuf,
    loc_sem, z_recv, z_send, x_recv, x_send,
    w_recv, w_send, wy_recv, wy_send, ws_recv, ws_send,
    y_recv, y_send, s_recv, s_send, t_recv, t_send, c_recv, c_send,
):
    b = lax.axis_index("blk")
    t = lax.axis_index("tp")
    c, y, h = b % 2, (b // 2) % 4, b // 8
    x, z = t % 4, t // 4
    part = b % 8
    xr, xl = (x + 1) % 4, (x + 3) % 4
    yr, yl, yo = (y + 1) % 4, (y + 3) % 4, (y + 2) % 4
    dev_xr, dev_xl = (b, z * 4 + xr), (b, z * 4 + xl)
    dev_yr, dev_yl = (h * 8 + yr * 2 + c, t), (h * 8 + yl * 2 + c, t)
    dev_sib = (b + 1 - 2 * c, t)
    zfar = (z + 2) % 4
    zhigh = z // 2
    h_up = (h + zhigh) % 2
    h_dn = (h + 1 - zhigh) % 2
    dev_up = (h_up * 8 + y * 2 + c, zfar * 4 + x)
    dev_dn = (h_dn * 8 + y * 2 + c, zfar * 4 + x)

    def rcopy(src, dst, ssem, rsem, dev):
        return pltpu.make_async_remote_copy(
            src_ref=src, dst_ref=dst, send_sem=ssem, recv_sem=rsem, device_id=dev, device_id_type=MESH
        )

    own_hid = pltpu.make_async_copy(hidden_ref, hid.at[z, x], loc_sem.at[0])
    own_hid.start()
    load_wq = pltpu.make_async_copy(wq_ref, wq, loc_sem.at[1])
    load_wq.start()

    barrier = pltpu.get_barrier_semaphore()

    def greet(dev):
        pl.semaphore_signal(barrier, inc=1, device_id=dev, device_id_type=MESH)

    def greet_tp(i, carry):
        greet((b, (t + i) % NT))
        return carry

    lax.fori_loop(1, NT, greet_tp, 0)
    for dev in (dev_yr, dev_yl, dev_sib, dev_up, dev_dn):
        greet(dev)
    pl.semaphore_wait(barrier, NT - 1 + 5)

    def rows(r):
        return pl.ds(r * RC, RC)

    def zk(k):
        return (z, z + 1 - 2 * (z % 2), 2 - z // 2, 3 - 3 * (z // 2))[k]

    def z_copy(r, zp, up):
        ref = hid.at[zp, x, rows(r)]
        g = r * 4 + zp
        to = (b, t + 4) if up else (b, t - 4)
        return rcopy(ref, ref, z_send.at[0 if up else 1, g], z_recv.at[g], to)

    def x_copy(r, zp, kind):
        g = r * 4 + zp
        if kind == 0:
            ref, to = hid.at[zp, x, rows(r)], dev_xr
        elif kind == 1:
            ref, to = hid.at[zp, x, rows(r)], dev_xl
        elif kind == 2:
            ref, to = hid.at[zp, xl, pl.ds(r * RC, HC)], dev_xr
        else:
            ref, to = hid.at[zp, xr, pl.ds(r * RC + HC, HC)], dev_xl
        return rcopy(ref, ref, x_send.at[kind, g], x_recv.at[kind, g], to)

    def x_wait(r, zp, kind):
        g = r * 4 + zp
        if kind == 0:
            ref, to = hid.at[zp, xl, rows(r)], dev_xl
        elif kind == 1:
            ref, to = hid.at[zp, xr, rows(r)], dev_xr
        elif kind == 2:
            ref, to = hid.at[zp, (x + 2) % 4, pl.ds(r * RC, HC)], dev_xl
        else:
            ref, to = hid.at[zp, (x + 2) % 4, pl.ds(r * RC + HC, HC)], dev_xr
        rcopy(ref, ref, x_send.at[kind, g], x_recv.at[kind, g], to).wait_recv()

    def a_send(n):
        r, k = n // 4, n % 4
        zp = zk(k)
        if k > 0:
            ref = hid.at[zp, x, rows(r)]
            g = r * 4 + zp
            rcopy(ref, ref, z_send.at[0, g], z_recv.at[g], dev_xr).wait_recv()
        x_copy(r, zp, 0).start()
        x_copy(r, zp, 1).start()

        @pl.when((z < 3) & (zp <= z))
        def _():
            z_copy(r, zp, True).start()

        @pl.when((z > 0) & (zp >= z))
        def _():
            z_copy(r, zp, False).start()

    def a_forward(n):
        r, k = n // 4, n % 4
        zp = zk(k)
        x_wait(r, zp, 0)
        x_copy(r, zp, 2).start()
        x_wait(r, zp, 1)
        x_copy(r, zp, 3).start()

    def a_finish(n):
        r, k = n // 4, n % 4
        zp = zk(k)
        x_wait(r, zp, 2)
        x_wait(r, zp, 3)

    def a_drain():
        for r in range(R):
            for zp in range(4):
                for kind in range(4):
                    x_copy(r, zp, kind).wait_send()

                @pl.when((z < 3) & (zp <= z))
                def _():
                    z_copy(r, zp, True).wait_send()

                @pl.when((z > 0) & (zp >= z))
                def _():
                    z_copy(r, zp, False).wait_send()

    def w_start():
        src_rows = pl.ds(part * PART, PART)

        def one(i, carry):
            to = (t + i) % NT
            rcopy(
                wkv_ref.at[src_rows, pl.ds(pl.multiple_of((to // 2) * 2 * HD, 2 * HD), 2 * HD)],
                wkv.at[t, part], w_send.at[0], w_recv.at[0], (b, to),
            ).start()
            return carry

        pltpu.make_async_copy(
            wkv_ref.at[src_rows, pl.ds(pl.multiple_of((t // 2) * 2 * HD, 2 * HD), 2 * HD)],
            wkv.at[t, part], w_recv.at[0],
        ).start()
        lax.fori_loop(1, NT, one, 0)

    def w_ref(p):
        return wkv.at[:, p]

    def w_copy(kind):
        if kind == 0:
            ref, to = wkv.at[:, part], dev_yr
        elif kind == 1:
            ref, to = wkv.at[:, part], dev_yl
        elif kind == 2:
            ref, to = wkv.at[pl.ds(0, 8), yl * 2 + c], dev_yr
        else:
            ref, to = wkv.at[pl.ds(8, 8), yr * 2 + c], dev_yl
        return rcopy(ref, ref, wy_send.at[kind], wy_recv.at[kind], to)

    def w_wait(kind):
        if kind == 0:
            ref = wkv.at[:, yl * 2 + c]
        elif kind == 1:
            ref = wkv.at[:, yr * 2 + c]
        elif kind == 2:
            ref = wkv.at[pl.ds(0, 8), yo * 2 + c]
        else:
            ref = wkv.at[pl.ds(8, 8), yo * 2 + c]
        rcopy(ref, ref, wy_send.at[kind], wy_recv.at[kind], dev_yl).wait_recv()

    def w_sib(i, mine=True):
        yy = (y, yl, yr, yo)[i]
        ref = wkv.at[:, yy * 2 + (c if mine else 1 - c)]
        return rcopy(ref, ref, ws_send.at[i], ws_recv.at[i], dev_sib)

    def w_step(i):
        if i == 0:
            ref = wkv.at[:, part]
            rcopy(ref, ref, w_send.at[0], w_recv.at[0], dev_xr).wait_recv()
            w_copy(0).start()
            w_copy(1).start()
            w_sib(0).start()
        elif i == 1:
            w_wait(0)
            w_copy(2).start()
            w_sib(1).start()
            w_wait(1)
            w_copy(3).start()
            w_sib(2).start()
        elif i == 2:
            w_wait(2)
            w_wait(3)
            w_sib(3).start()
        else:
            for j in range(4):
                w_sib(j, False).wait_recv()

    def w_drain():
        ref = wkv.at[pl.ds(0, NT - 1), part]
        rcopy(ref, ref, w_send.at[0], w_recv.at[0], dev_xr).wait_send()
        for j in range(4):
            w_copy(j).wait_send()
            w_sib(j).wait_send()

    def project(r):
        acc[...] = jnp.zeros_like(acc)

        def body(zp, carry):
            for half in range(2):
                total = None
                for xp in range(4):
                    rhs = wq[zp * 4 + xp] if half == 0 else wkv[zp * 4 + xp].reshape(FD, 2 * HD)
                    one = jnp.dot(hid[zp, xp, rows(r)], rhs, preferred_element_type=jnp.float32)
                    total = one if total is None else total + one
                acc[half] += total
            return carry

        lax.fori_loop(0, 4, body, 0)
        qbuf[rows(r)] = acc[0].astype(jnp.bfloat16)
        kv[b, rows(r)] = acc[1].astype(jnp.bfloat16)

    def kv_block(far, yy, cc):
        return ((h + far) % 2) * 8 + yy * 2 + cc

    def b_copy(r, far, kind):
        if kind == 0:
            ref, to = kv.at[kv_block(far, y, c), rows(r)], dev_yr
        elif kind == 1:
            ref, to = kv.at[kv_block(far, y, c), rows(r)], dev_yl
        elif kind == 2:
            ref, to = kv.at[kv_block(far, yl, c), pl.ds(r * RC, HC)], dev_yr
        else:
            ref, to = kv.at[kv_block(far, yr, c), pl.ds(r * RC + HC, HC)], dev_yl
        g = r * 2 + far
        return rcopy(ref, ref, y_send.at[kind, g], y_recv.at[kind, g], to)

    def b_wait(r, far, kind):
        if kind == 0:
            ref = kv.at[kv_block(far, yl, c), rows(r)]
        elif kind == 1:
            ref = kv.at[kv_block(far, yr, c), rows(r)]
        elif kind == 2:
            ref = kv.at[kv_block(far, yo, c), pl.ds(r * RC, HC)]
        else:
            ref = kv.at[kv_block(far, yo, c), pl.ds(r * RC + HC, HC)]
        g = r * 2 + far
        rcopy(ref, ref, y_send.at[kind, g], y_recv.at[kind, g], dev_yl).wait_recv()

    def b_sib(r, far, i, mine=True):
        yy = (y, yl, yr, yo)[i]
        ref = kv.at[kv_block(far, yy, c if mine else 1 - c), rows(r)]
        g = r * 2 + far
        return rcopy(ref, ref, s_send.at[i, g], s_recv.at[i, g], dev_sib)

    def cross_first(r, way):
        src = kv.at[b, pl.ds(r * RC + way * HC, HC)]
        return rcopy(
            src, tmp.at[r, way], t_send.at[r, way], t_recv.at[r, way], (dev_up, dev_dn)[way]
        )

    def cross_second(r, way):
        hs = (h_dn, h_up)[way]
        dst = kv.at[hs * 8 + y * 2 + c, pl.ds(r * RC + way * HC, HC)]
        return rcopy(
            tmp.at[r, way], dst, c_send.at[r, way], c_recv.at[r, way], (dev_up, dev_dn)[way]
        )

    def cross_wait(r, way):
        dst = kv.at[kv_block(1, y, c), pl.ds(r * RC + way * HC, HC)]
        rcopy(
            tmp.at[r, way], dst, c_send.at[r, way], c_recv.at[r, way], (dev_up, dev_dn)[way]
        ).wait_recv()

    def b_step(r, i):
        if i == 0:
            for way in range(2):
                cross_first(r, way).start()
            b_copy(r, 0, 0).start()
            b_copy(r, 0, 1).start()
            b_sib(r, 0, 0).start()
        elif i == 1:
            for way in range(2):
                cross_first(r, way).wait_recv()
                cross_second(r, way).start()
            b_forward(r, 0)
        elif i == 2:
            b_finish(r, 0)
            for way in range(2):
                cross_wait(r, way)
            b_copy(r, 1, 0).start()
            b_copy(r, 1, 1).start()
            b_sib(r, 1, 0).start()
        elif i == 3:
            b_forward(r, 1)
        elif i == 4:
            b_finish(r, 1)
        else:
            for far in range(2):
                for j in range(4):
                    b_sib(r, far, j, False).wait_recv()

    def b_forward(r, far):
        b_wait(r, far, 0)
        b_copy(r, far, 2).start()
        b_sib(r, far, 1).start()
        b_wait(r, far, 1)
        b_copy(r, far, 3).start()
        b_sib(r, far, 2).start()

    def b_finish(r, far):
        b_wait(r, far, 2)
        b_wait(r, far, 3)
        b_sib(r, far, 3).start()

    def b_drain():
        for r in range(R):
            for far in range(2):
                for j in range(4):
                    b_copy(r, far, j).wait_send()
                    b_sib(r, far, j).wait_send()
            for way in range(2):
                cross_first(r, way).wait_send()
                cross_second(r, way).wait_send()

    own_hid.wait()
    for n in range(4 * R + 6):
        if n < 4 * R:
            a_send(n)
        if n == 0:
            w_start()
        if 1 <= n <= 4 * R:
            a_forward(n - 1)
        if 2 <= n <= 4 * R + 1:
            a_finish(n - 2)
        if 1 <= n <= 3:
            w_step(n - 1)
        if n == 5:
            w_step(3)
            load_wq.wait()
        if n >= 5 and (n - 5) % 4 == 0 and n < 4 * R + 5:
            project((n - 5) // 4)
        for r in range(R):
            i = n - (4 * r + 5)
            if 0 <= i <= 4:
                b_step(r, i)
    for r in range(R):
        b_step(r, 5)

    count = jnp.int32(0)
    index = [jnp.int32(0)] * CAP
    for bb in range(NB):
        hit = hosts_ref[routing_ref[bb]] == b
        for s in range(CAP):
            index[s] = jnp.where(hit & (count == s), bb, index[s])
        count = count + hit.astype(jnp.int32)
    for s in range(CAP):
        @pl.when(t % 2 == 0)
        def _():
            cbuf[s] = jnp.where(s < count, kv[index[s], :, 0:HD], jnp.zeros((TOK, HD), jnp.bfloat16))

        @pl.when(t % 2 == 1)
        def _():
            cbuf[s] = jnp.where(s < count, kv[index[s], :, HD:], jnp.zeros((TOK, HD), jnp.bfloat16))
    store_cache = pltpu.make_async_copy(cbuf, cache_ref, loc_sem.at[2])
    store_cache.start()

    lanes = TOK // HD

    def lane_max(m, s):
        for i in range(lanes):
            m = jnp.maximum(m, s[:, i * HD : (i + 1) * HD])
        return m

    def q_tile(i, carry):
        r0 = pl.multiple_of(i * TQ, TQ)
        q = jnp.concatenate([qbuf[pl.ds(r0, TQ), 0:HD], qbuf[pl.ds(r0, TQ), HD:]], axis=0)

        def scores(kb):
            return lax.dot_general(
                q, kv[kb, :, 0:HD], (((1,), (1,)), ((), ())), preferred_element_type=jnp.float32
            )

        def first(kb, m):
            s = scores(kb)
            sbuf[kb] = s
            return lane_max(m, s)

        m = lax.fori_loop(0, b, first, jnp.full((2 * TQ, HD), NEG, jnp.float32))
        s = scores(b)
        row = lax.broadcasted_iota(jnp.int32, (2 * TQ, TOK), 0) % TQ + r0
        col = lax.broadcasted_iota(jnp.int32, (2 * TQ, TOK), 1)
        s = jnp.where(col <= row, s, NEG)
        sbuf[b] = s
        m = jnp.max(lane_max(m, s), axis=1, keepdims=True) * SCALE2

        def second(kb, state):
            total, out = state
            p = jnp.exp2(sbuf[kb] * SCALE2 - m)
            for j in range(lanes):
                total = total + p[:, j * HD : (j + 1) * HD]
            out = out + jnp.dot(
                p.astype(jnp.bfloat16), kv[kb, :, HD:], preferred_element_type=jnp.float32
            )
            return total, out

        zero = jnp.zeros((2 * TQ, HD), jnp.float32)
        total, out = lax.fori_loop(0, b + 1, second, (zero, zero))
        out = (out / jnp.sum(total, axis=1, keepdims=True)).astype(jnp.bfloat16)
        att_ref[pl.ds(r0, TQ), 0:HD] = out[:TQ]
        att_ref[pl.ds(r0, TQ), HD:] = out[TQ:]
        return carry

    lax.fori_loop(0, TOK // TQ, q_tile, 0)

    a_drain()
    w_drain()
    b_drain()
    store_cache.wait()


def local(hidden_in, w_query, w_keyval, routing, hosts):
    any_spec = pl.BlockSpec(memory_space=pl.ANY)
    smem = pl.BlockSpec(memory_space=pltpu.SMEM)
    dma = pltpu.SemaphoreType.DMA
    bf16, f32 = jnp.bfloat16, jnp.float32
    attended, cache = pl.pallas_call(
        kernel,
        out_shape=(
            jax.ShapeDtypeStruct((TOK, 2 * HD), bf16),
            jax.ShapeDtypeStruct((CAP, TOK, HD), bf16),
        ),
        in_specs=[any_spec, any_spec, any_spec, smem, smem],
        out_specs=(pl.BlockSpec(memory_space=pltpu.VMEM), any_spec),
        scratch_shapes=[
            pltpu.VMEM((4, 4, TOK, FD), bf16),
            pltpu.VMEM((NT, FD, 2 * HD), bf16),
            pltpu.VMEM((NT, 8, PART, 2 * HD), bf16),
            pltpu.VMEM((NB, TOK, 2 * HD), bf16),
            pltpu.VMEM((R, 2, HC, 2 * HD), bf16),
            pltpu.VMEM((2, RC, 2 * HD), f32),
            pltpu.VMEM((TOK, 2 * HD), bf16),
            pltpu.VMEM((NB, 2 * TQ, TOK), f32),
            pltpu.VMEM((CAP, TOK, HD), bf16),
            dma((3,)),
            dma((4 * R,)), dma((2, 4 * R)),
            dma((4, 4 * R)), dma((4, 4 * R)),
            dma((1,)), dma((1,)),
            dma((4,)), dma((4,)),
            dma((4,)), dma((4,)),
            dma((4, 2 * R)), dma((4, 2 * R)),
            dma((4, 2 * R)), dma((4, 2 * R)),
            dma((R, 2)), dma((R, 2)),
            dma((R, 2)), dma((R, 2)),
        ],
        compiler_params=pltpu.CompilerParams(
            collective_id=0, has_side_effects=True, vmem_limit_bytes=56 * 1024 * 1024
        ),
        cost_estimate=pl.CostEstimate(flops=8 * 10**9, bytes_accessed=8 * 2**20, transcendentals=8 * 2**20),
    )(hidden_in, w_query.reshape(NT, FD, 2 * HD), w_keyval, routing.reshape(NB), hosts)
    return attended, cache[None]


def solution(mesh):
    in_specs = (P("blk", "tp"), P(None, "tp"), P("tp", None), P(), P())
    out_specs = (P("blk", "tp"), P("blk", None, None, "tp"))
    return jax.shard_map(local, mesh=mesh, in_specs=in_specs, out_specs=out_specs, check_vma=False)
```

time: 443 us -> 110 us (0.25)
  the two profiles are of different devices: /device:TPU:1 before, /device:TPU:153 now
where the time goes in v1:
time: 110 us
  Pallas kernels  105 us (95%)
  local copies, waits for them, and re-layouts  3.94 us (4%)
    pallas_call x1, Pallas kernels, local(): pl.pallas_call(kernel, out_shape=(jax.ShapeDtypeStruct((TOK, 2 * HD), bf1...  105 us
    unnamed x2, local copies, waits for them, and re-layouts  3.94 us

profile of v1, /device:TPU:153, one launch (start us, length us, event | category | flops | bytes accessed | tf_op | source)
XLA Modules:
  0.0 109.6 jit_solution(4198265329738737477)
XLA Ops:
  0.6 105.0 %shard_map.68 = (bf16[512,256]{1,0:T(8,128)(2,1)}, bf16[8,512,128]{2,1,0:T(8,128)(2,1)}) custom-call(bf16[512,256]{1,0:T(8,128)(2,1)} %hidden_ref.1, bf16[16,256,256]{2,1,0:T(8,128)(2,1)} %bitcast.4, bf16[256,2048]{1,0:T(8,128)(2,1)} %wkv_ref.1, s32[16]{0:T(128)} %bitcast.5, s32[16]{0:T(128)} %hosts_ref.1), custom_call_target="tpu_custom_call" | custom-call | flops 8000000000 | bytes 8388608 | tf_op jit(solution)/shard_map/pallas_call | solution.py:457
  105.6 1.7 %copy.9 = bf16[512,256]{1,0:T(8,128)(2,1)} copy(bf16[512,256]{1,0:T(8,128)(2,1)} %get-tuple-element.8) | data formatting | bytes 524288
  107.3 2.3 %copy.10 = bf16[1,8,512,128]{3,2,1,0:T(8,128)(2,1)} copy(bf16[1,8,512,128]{3,2,1,0:T(8,128)(2,1)} %bitcast.3) | data formatting | bytes 2097152

commit v2 on v0

v2 whole, which is shorter than its diff:
```python
import functools

import jax
import jax.numpy as jnp
from jax import lax
from jax.experimental import pallas as pl
from jax.experimental.pallas import tpu as pltpu
from jax.sharding import PartitionSpec as P

HEADS = 32
KVH = 8
HD = 128
TOK = 512
CAP = 8
NB = 16
NT = 16
FD = 256
PART = 32
R = 4
RC = TOK // R
HC = RC // 2
TILE = 2 * TOK // 2
QUAD = 4
MESH = pl.DeviceIdType.MESH
LOG2E = 1.4426950408889634
SCALE2 = HD**-0.5 * LOG2E
NEG = -1e30

XSEQ = [
    (0, 0), (1, 0), (0, 1), (1, 1), (0, 2), (2, 0), (0, 3), (1, 2),
    (1, 3), (3, 0), (2, 1), (2, 2), (2, 3), (3, 1), (3, 2), (3, 3),
]
LAG = 2


def steps():
    at = {3: ["w0"], 8: ["w1"], 10: ["w2"], 11: ["p0"], 13: ["p1"], 15: ["b0.1"]}
    order = ["s0"]
    for s in range(len(XSEQ)):
        if s > 0:
            order.append(f"s{s}")
        if s == 0:
            order.append("w")
        if s + 1 < len(XSEQ):
            order.append(f"z{s + 1}")
        if s >= LAG:
            order.append(f"f{s - LAG}")
        order += at.get(s, [])
    order += [f"f{s}" for s in range(len(XSEQ) - LAG, len(XSEQ) - 1)]
    order += ["p2", "b1.1", "b0.2", "b0.3", "p3", "u0.0", "b1.2", "u1.0", "b1.3", "b2.1", "u0.1", "u1.1"]
    order += ["b2.2", "b3.1", "b2.3", "u0.2", "u1.2", "b3.2", "b3.3"]
    return order


def kernel(
    hidden_ref, wq_ref, wkv_ref, routing_ref, hosts_ref,
    att_ref, cache_ref,
    hid, wq, wkv, kv, acc, qbuf, sbuf, mbuf, lbuf, abuf, cbuf,
    loc_sem, z_recv, z_send, x_recv, xh_recv, x_send,
    w_recv, w_send, wy_recv, wy_send, ws_recv, ws_send,
    y_recv, y_send, s_recv, s_send, c_recv, c_send, a_sem,
):
    b = lax.axis_index("blk")
    t = lax.axis_index("tp")
    c, y, h = b % 2, (b // 2) % 4, b // 8
    x, z = t % 4, t // 4
    part = b % 8
    xr, xl, xo = (x + 1) % 4, (x + 3) % 4, (x + 2) % 4
    yr, yl, yo = (y + 1) % 4, (y + 3) % 4, (y + 2) % 4
    dev_xr, dev_xl = (b, z * 4 + xr), (b, z * 4 + xl)
    dev_y = [(h * 8 + yy * 2 + c, t) for yy in (yr, yl, yo)]
    dev_xo = (b, z * 4 + xo)
    dev_sib = (b + 1 - 2 * c, t)
    dev_far = ((1 - h) * 8 + y * 2 + c, t)

    def rcopy(src, dst, ssem, rsem, dev):
        return pltpu.make_async_remote_copy(
            src_ref=src, dst_ref=dst, send_sem=ssem, recv_sem=rsem, device_id=dev, device_id_type=MESH
        )

    def recv(ref, rsem):
        rcopy(ref, ref, x_send.at[0], rsem, dev_xr).wait_recv()

    def sent(ref, ssem):
        rcopy(ref, ref, ssem, w_recv.at[0], dev_xr).wait_send()

    own_hid = pltpu.make_async_copy(hidden_ref, hid.at[z, x], loc_sem.at[0])
    own_hid.start()
    load_wq = pltpu.make_async_copy(wq_ref, wq, loc_sem.at[1])
    load_wq.start()

    barrier = pltpu.get_barrier_semaphore()

    def greet(dev):
        pl.semaphore_signal(barrier, inc=1, device_id=dev, device_id_type=MESH)

    def greet_tp(i, carry):
        greet((b, (t + i) % NT))
        return carry

    lax.fori_loop(1, NT, greet_tp, 0)
    for dev in (*dev_y, dev_sib, dev_far):
        greet(dev)
    pl.semaphore_wait(barrier, NT - 1 + 5)

    def rows(r):
        return pl.ds(r * RC, RC)

    def half(r, i):
        return pl.ds(r * RC + i * HC, HC)

    def zk(k):
        return (z, z + 1 - 2 * (z % 2), 2 - z // 2, 3 - 3 * (z // 2))[k]

    def piece_of(s):
        r, k = XSEQ[s]
        zp = zk(k)
        return r, zp, r * 4 + zp

    def z_step(s):
        r, zp, g = piece_of(s)
        ref = hid.at[zp, x, rows(r)]
        if XSEQ[s][1] > 0:
            recv(ref, z_recv.at[g])

        @pl.when((z < 3) & (zp <= z))
        def _():
            rcopy(ref, ref, z_send.at[0, zp], z_recv.at[g], (b, t + 4)).start()

        @pl.when((z > 0) & (zp >= z))
        def _():
            rcopy(ref, ref, z_send.at[1, zp], z_recv.at[g], (b, t - 4)).start()

    def a_send(s):
        r, zp, g = piece_of(s)
        ref = hid.at[zp, x, rows(r)]
        rcopy(ref, ref, x_send.at[0], x_recv.at[0, g], dev_xr).start()
        rcopy(ref, ref, x_send.at[1], x_recv.at[1, g], dev_xl).start()
        if s == len(XSEQ) - 1:
            rcopy(ref, ref, x_send.at[2], xh_recv.at[r], dev_xo).start()

    def a_forward(s):
        r, zp, g = piece_of(s)
        recv(hid.at[zp, xl, rows(r)], x_recv.at[0, g])
        ref = hid.at[zp, xl, half(r, 0)]
        rcopy(ref, ref, x_send.at[2], xh_recv.at[r], dev_xr).start()
        recv(hid.at[zp, xr, rows(r)], x_recv.at[1, g])
        ref = hid.at[zp, xr, half(r, 1)]
        rcopy(ref, ref, x_send.at[3], xh_recv.at[r], dev_xl).start()

    def a_finish(r):
        recv(hid.at[:, xo, rows(r)], xh_recv.at[r])
        if r == R - 1:
            _, zp, g = piece_of(len(XSEQ) - 1)
            recv(hid.at[zp, xl, rows(r)], x_recv.at[0, g])
            recv(hid.at[zp, xr, rows(r)], x_recv.at[1, g])

    def a_drain():
        for kind in range(2):
            sent(hid.at[:, x], x_send.at[kind])
        sent(hid.at[pl.ds(0, 2), x], x_send.at[2])
        sent(hid.at[0, x, pl.ds(0, HC)], x_send.at[2])
        sent(hid.at[0, x], x_send.at[3])
        sent(hid.at[0, x, pl.ds(0, 3 * RC + HC)], x_send.at[3])
        for zp in range(4):
            @pl.when((z < 3) & (zp <= z))
            def _():
                sent(hid.at[zp, x], z_send.at[0, zp])

            @pl.when((z > 0) & (zp >= z))
            def _():
                sent(hid.at[zp, x], z_send.at[1, zp])

    def w_start():
        src_rows = pl.ds(part * PART, PART)

        def piece(to):
            return wkv_ref.at[src_rows, pl.ds(pl.multiple_of((to // 2) * 2 * HD, 2 * HD), 2 * HD)]

        def one(i, carry):
            to = (t + i) % NT
            rcopy(piece(to), wkv.at[t, y, c], w_send.at[0], w_recv.at[0], (b, to)).start()
            return carry

        pltpu.make_async_copy(piece(t), wkv.at[t, y, c], w_recv.at[0]).start()
        lax.fori_loop(1, NT, one, 0)

    def w_step(i):
        if i == 0:
            ref = wkv.at[:, y, c]
            recv(ref, w_recv.at[0])
            for j in range(3):
                rcopy(ref, ref, wy_send.at[0], wy_recv.at[0], dev_y[j]).start()
        elif i == 1:
            recv(wkv.at[:, pl.ds(0, 3), c], wy_recv.at[0])
            ref = wkv.at[:, :, c]
            rcopy(ref, ref, ws_send.at[0], ws_recv.at[0], dev_sib).start()
        else:
            recv(wkv.at[:, :, 1 - c], ws_recv.at[0])

    def w_drain():
        sent(wkv.at[pl.ds(0, NT - 1), y, c], w_send.at[0])
        sent(wkv.at[:, pl.ds(0, 3), c], wy_send.at[0])
        sent(wkv.at[:, :, c], ws_send.at[0])

    def project(r):
        acc[...] = jnp.zeros_like(acc)

        def body(zp, carry):
            for side in range(2):
                total = None
                for xp in range(4):
                    rhs = wq[zp * 4 + xp] if side == 0 else wkv[zp * 4 + xp].reshape(FD, 2 * HD)
                    one = jnp.dot(hid[zp, xp, rows(r)], rhs, preferred_element_type=jnp.float32)
                    total = one if total is None else total + one
                acc[side] += total
            return carry

        lax.fori_loop(0, 4, body, 0)
        kv[h, y, c, rows(r)] = acc[1].astype(jnp.bfloat16)
        for head in range(2):
            at = (r // 2) * TILE + head * (TILE // 2) + (r % 2) * RC
            qbuf[pl.ds(at, RC)] = acc[0, :, head * HD : (head + 1) * HD].astype(jnp.bfloat16)

    def b_send(r, far):
        ref = kv.at[(h + far) % 2, y, c, rows(r)]
        for j in range(3):
            rcopy(ref, ref, y_send.at[0], y_recv.at[r, far], dev_y[j]).start()

    def b_share(r, far):
        recv(kv.at[0, pl.ds(0, 3), c, rows(r)], y_recv.at[r, far])
        ref = kv.at[(h + far) % 2, :, c, rows(r)]
        rcopy(ref, ref, s_send.at[0], s_recv.at[r], dev_sib).start()

    def b_step(r, i):
        if i == 0:
            ref = kv.at[h, y, c, rows(r)]
            rcopy(ref, ref, c_send.at[0], c_recv.at[r], dev_far).start()
            b_send(r, 0)
        elif i == 1:
            recv(kv.at[1 - h, y, c, rows(r)], c_recv.at[r])
            b_send(r, 1)
            b_share(r, 0)
        elif i == 2:
            b_share(r, 1)
        else:
            recv(kv.at[:, :, 1 - c, rows(r)], s_recv.at[r])

    def b_drain():
        sent(kv.at[0, pl.ds(0, 3)], y_send.at[0])
        sent(kv.at[:, :, 0], s_send.at[0])
        sent(kv.at[0, 0, 0], c_send.at[0])

    quads = b // QUAD

    def quad_of(p, r, first):
        return kv[p // 2, pl.ds((p % 2) * 2, 2), :, rows(r), first : first + HD].reshape(QUAD * RC, HD)

    def unit(i, r):
        at = pl.ds(i * TILE, TILE)
        q = qbuf[at]
        start = jnp.full((TILE, HD), NEG, jnp.float32) if r == 0 else mbuf[i, r - 1]

        def scores(p):
            return SCALE2 * lax.dot_general(
                q, quad_of(p, r, 0), (((1,), (1,)), ((), ())), preferred_element_type=jnp.float32
            )

        def keep(p, s, m):
            sbuf[i, r, p] = s
            for j in range(QUAD):
                m = jnp.maximum(m, s[:, j * RC : (j + 1) * RC])
            return m

        m = lax.fori_loop(0, quads, lambda p, m: keep(p, scores(p), m), start)
        row = lax.broadcasted_iota(jnp.int32, (TILE, QUAD * RC), 0) % (TILE // 2) + (b * TOK + i * (TILE // 2))
        col = lax.broadcasted_iota(jnp.int32, (TILE, QUAD * RC), 1)
        col = col % RC + (col // RC) * TOK + (quads * QUAD * TOK + r * RC)
        m = keep(quads, jnp.where(col <= row, scores(quads), NEG), m)
        m = jnp.broadcast_to(jnp.max(m, axis=1, keepdims=True), (TILE, HD))
        mbuf[i, r] = m

        def exps(p, total):
            s = sbuf[i, r, p]
            e = [jnp.exp2(s[:, j * RC : (j + 1) * RC] - m) for j in range(QUAD)]
            sbuf[i, r, p] = jnp.concatenate(e, axis=1)
            return total + ((e[0] + e[1]) + (e[2] + e[3]))

        total = jnp.zeros((TILE, HD), jnp.float32) if r == 0 else lbuf[i] * jnp.exp2(start - m)
        lbuf[i] = lax.fori_loop(0, quads + 1, exps, total)

    def values(i):
        final = mbuf[i, R - 1]
        out = jnp.zeros((TILE, HD), jnp.float32)
        for r in range(R):
            factor = None if r == R - 1 else jnp.exp2(mbuf[i, r] - final)

            def body(p, out):
                e = sbuf[i, r, p]
                if factor is not None:
                    e = jnp.concatenate([e[:, j * RC : (j + 1) * RC] * factor for j in range(QUAD)], axis=1)
                return out + jnp.dot(
                    e.astype(jnp.bfloat16), quad_of(p, r, HD), preferred_element_type=jnp.float32
                )

            out = lax.fori_loop(0, quads + 1, body, out)
        out = (out / jnp.sum(lbuf[i], axis=1, keepdims=True)).astype(jnp.bfloat16)
        at = pl.ds(i * (TILE // 2), TILE // 2)
        abuf[at, 0:HD] = out[: TILE // 2]
        abuf[at, HD:] = out[TILE // 2 :]
        pltpu.make_async_copy(abuf.at[at], att_ref.at[at], a_sem.at[0]).start()

    own_hid.wait()
    for step in steps():
        what, number = step[0], step[1:]
        if what == "s":
            if XSEQ[int(number)][1] == 0:
                z_step(int(number))
            a_send(int(number))
        elif what == "z":
            if XSEQ[int(number)][1] > 0:
                z_step(int(number))
        elif what == "f":
            a_forward(int(number))
        elif what == "w":
            w_step(int(number)) if number else w_start()
        elif what == "p":
            r = int(number)
            if r == 0:
                load_wq.wait()
            a_finish(r)
            project(r)
            b_step(r, 0)
        elif what == "b":
            b_step(int(number[0]), int(number[2]))
        else:
            unit(int(number[0]), int(number[2]))
    for i in range(2):
        unit(i, R - 1)

    count = jnp.int32(0)
    index = [jnp.int32(0)] * CAP
    for bb in range(NB):
        hit = hosts_ref[routing_ref[bb]] == b
        for s in range(CAP):
            index[s] = jnp.where(hit & (count == s), bb, index[s])
        count = count + hit.astype(jnp.int32)
    for s in range(CAP):
        @pl.when(t % 2 == 0)
        def _():
            cbuf[s] = jnp.where(s < count, kv[index[s] // 8, (index[s] // 2) % 4, index[s] % 2, :, 0:HD], jnp.zeros((TOK, HD), jnp.bfloat16))

        @pl.when(t % 2 == 1)
        def _():
            cbuf[s] = jnp.where(s < count, kv[index[s] // 8, (index[s] // 2) % 4, index[s] % 2, :, HD:], jnp.zeros((TOK, HD), jnp.bfloat16))
    store_cache = pltpu.make_async_copy(cbuf, cache_ref, loc_sem.at[2])
    store_cache.start()

    for i in range(2):
        values(i)

    a_drain()
    w_drain()
    b_drain()
    store_cache.wait()
    pltpu.make_async_copy(abuf, att_ref, a_sem.at[0]).wait()


def local(hidden_in, w_query, w_keyval, routing, hosts):
    any_spec = pl.BlockSpec(memory_space=pl.ANY)
    smem = pl.BlockSpec(memory_space=pltpu.SMEM)
    dma = pltpu.SemaphoreType.DMA
    bf16, f32 = jnp.bfloat16, jnp.float32
    attended, cache = pl.pallas_call(
        kernel,
        out_shape=(
            jax.ShapeDtypeStruct((TOK, 2 * HD), bf16),
            jax.ShapeDtypeStruct((CAP, TOK, HD), bf16),
        ),
        in_specs=[any_spec, any_spec, any_spec, smem, smem],
        out_specs=(any_spec, any_spec),
        scratch_shapes=[
            pltpu.VMEM((4, 4, TOK, FD), bf16),
            pltpu.VMEM((NT, FD, 2 * HD), bf16),
            pltpu.VMEM((NT, 4, 2, PART, 2 * HD), bf16),
            pltpu.VMEM((2, 4, 2, TOK, 2 * HD), bf16),
            pltpu.VMEM((2, RC, 2 * HD), f32),
            pltpu.VMEM((2 * TILE, HD), bf16),
            pltpu.VMEM((2, R, NB // QUAD, TILE, QUAD * RC), f32),
            pltpu.VMEM((2, R, TILE, HD), f32),
            pltpu.VMEM((2, TILE, HD), f32),
            pltpu.VMEM((TOK, 2 * HD), bf16),
            pltpu.VMEM((CAP, TOK, HD), bf16),
            dma((3,)),
            dma((4 * R,)), dma((2, 4)),
            dma((2, 4 * R)), dma((R,)), dma((4,)),
            dma((1,)), dma((1,)),
            dma((1,)), dma((1,)),
            dma((1,)), dma((1,)),
            dma((R, 2)), dma((1,)),
            dma((R,)), dma((1,)),
            dma((R,)), dma((1,)),
            dma((1,)),
        ],
        compiler_params=pltpu.CompilerParams(
            collective_id=0, has_side_effects=True, vmem_limit_bytes=58 * 1024 * 1024
        ),
        cost_estimate=pl.CostEstimate(flops=8 * 10**9, bytes_accessed=8 * 2**20, transcendentals=8 * 2**20),
    )(hidden_in, w_query.reshape(NT, FD, 2 * HD), w_keyval, routing.reshape(NB), hosts)
    return attended, cache[None]


def solution(mesh):
    in_specs = (P("blk", "tp"), P(None, "tp"), P("tp", None), P(), P())
    out_specs = (P("blk", "tp"), P("blk", None, None, "tp"))
    return jax.shard_map(local, mesh=mesh, in_specs=in_specs, out_specs=out_specs, check_vma=False)
```

time: 443 us -> 90.5 us (0.20)
  the two profiles are of different devices: /device:TPU:1 before, /device:TPU:153 now
where the time goes in v2:
time: 90.5 us; the launch traced here: 89.5 us
  Pallas kernels  84.9 us (94%)
  local copies, waits for them, and re-layouts  3.94 us (4%)
    pallas_call x1, Pallas kernels, local(): pl.pallas_call(kernel, out_shape=(jax.ShapeDtypeStruct((TOK, 2 * HD), bf1...  84.9 us
    unnamed x2, local copies, waits for them, and re-layouts  3.94 us

profile of v2, /device:TPU:153, one launch (start us, length us, event | category | flops | bytes accessed | tf_op | source)
XLA Modules:
  0.0 89.5 jit_solution(15759541896499561363)
XLA Ops:
  0.6 84.9 %shard_map.68 = (bf16[512,256]{1,0:T(8,128)(2,1)}, bf16[8,512,128]{2,1,0:T(8,128)(2,1)}) custom-call(bf16[512,256]{1,0:T(8,128)(2,1)} %hidden_ref.1, bf16[16,256,256]{2,1,0:T(8,128)(2,1)} %bitcast.4, bf16[256,2048]{1,0:T(8,128)(2,1)} %wkv_ref.1, s32[16]{0:T(128)} %bitcast.5, s32[16]{0:T(128)} %hosts_ref.1), custom_call_target="tpu_custom_call" | custom-call | flops 8000000000 | bytes 8388608 | tf_op jit(solution)/shard_map/pallas_call | solution.py:374
  85.6 1.7 %copy.9 = bf16[512,256]{1,0:T(8,128)(2,1)} copy(bf16[512,256]{1,0:T(8,128)(2,1)} %get-tuple-element.8) | data formatting | bytes 524288
  87.2 2.3 %copy.10 = bf16[1,8,512,128]{3,2,1,0:T(8,128)(2,1)} copy(bf16[1,8,512,128]{3,2,1,0:T(8,128)(2,1)} %bitcast.3) | data formatting | bytes 2097152

commit v3 on v2

--- a/solution.py
+++ b/solution.py
@@ -48,7 +48,7 @@
         order += at.get(s, [])
     order += [f"f{s}" for s in range(len(XSEQ) - LAG, len(XSEQ) - 1)]
     order += ["p2", "b1.1", "b0.2", "b0.3", "p3", "u0.0", "b1.2", "u1.0", "b1.3", "b2.1", "u0.1", "u1.1"]
-    order += ["b2.2", "b3.1", "b2.3", "u0.2", "u1.2", "b3.2", "b3.3"]
+    order += ["b2.2", "b3.1k", "b3.1v", "b2.3", "u0.2", "u1.2", "b3.2k", "b3.2v", "b3.3k", "u0.3", "u1.3", "b3.3v"]
     return order
 
 
@@ -217,44 +217,53 @@
             return carry
 
         lax.fori_loop(0, 4, body, 0)
-        kv[h, y, c, rows(r)] = acc[1].astype(jnp.bfloat16)
+        for j in range(2):
+            kv[j, h, y, c, rows(r)] = acc[1, :, j * HD : (j + 1) * HD].astype(jnp.bfloat16)
         for head in range(2):
             at = (r // 2) * TILE + head * (TILE // 2) + (r % 2) * RC
             qbuf[pl.ds(at, RC)] = acc[0, :, head * HD : (head + 1) * HD].astype(jnp.bfloat16)
 
-    def b_send(r, far):
-        ref = kv.at[(h + far) % 2, y, c, rows(r)]
+    def sides(part):
+        return pl.ds(0, 2) if part == 2 else pl.ds(part, 1)
+
+    def slot(r, part):
+        return R if part == 1 else r
+
+    def b_send(r, part, far):
+        ref = kv.at[sides(part), (h + far) % 2, y, c, rows(r)]
         for j in range(3):
-            rcopy(ref, ref, y_send.at[0], y_recv.at[r, far], dev_y[j]).start()
-
-    def b_share(r, far):
-        recv(kv.at[0, pl.ds(0, 3), c, rows(r)], y_recv.at[r, far])
-        ref = kv.at[(h + far) % 2, :, c, rows(r)]
-        rcopy(ref, ref, s_send.at[0], s_recv.at[r], dev_sib).start()
-
-    def b_step(r, i):
+            rcopy(ref, ref, y_send.at[0], y_recv.at[slot(r, part), far], dev_y[j]).start()
+
+    def b_share(r, part, far):
+        hh = (h + far) % 2
+        recv(kv.at[sides(part), hh, pl.ds(0, 3), c, rows(r)], y_recv.at[slot(r, part), far])
+        ref = kv.at[sides(part), hh, :, c, rows(r)]
+        rcopy(ref, ref, s_send.at[0], s_recv.at[slot(r, part)], dev_sib).start()
+
+    def b_step(r, i, part=2):
+        at = slot(r, part)
         if i == 0:
-            ref = kv.at[h, y, c, rows(r)]
-            rcopy(ref, ref, c_send.at[0], c_recv.at[r], dev_far).start()
-            b_send(r, 0)
+            ref = kv.at[sides(part), h, y, c, rows(r)]
+            rcopy(ref, ref, c_send.at[0], c_recv.at[at], dev_far).start()
+            b_send(r, part, 0)
         elif i == 1:
-            recv(kv.at[1 - h, y, c, rows(r)], c_recv.at[r])
-            b_send(r, 1)
-            b_share(r, 0)
+            recv(kv.at[sides(part), 1 - h, y, c, rows(r)], c_recv.at[at])
+            b_send(r, part, 1)
+            b_share(r, part, 0)
         elif i == 2:
-            b_share(r, 1)
+            b_share(r, part, 1)
         else:
-            recv(kv.at[:, :, 1 - c, rows(r)], s_recv.at[r])
+            recv(kv.at[sides(part), :, :, 1 - c, rows(r)], s_recv.at[at])
 
     def b_drain():
-        sent(kv.at[0, pl.ds(0, 3)], y_send.at[0])
-        sent(kv.at[:, :, 0], s_send.at[0])
-        sent(kv.at[0, 0, 0], c_send.at[0])
+        sent(kv.at[:, 0, pl.ds(0, 3)], y_send.at[0])
+        sent(kv.at[:, :, :, 0], s_send.at[0])
+        sent(kv.at[:, 0, 0, 0], c_send.at[0])
 
     quads = b // QUAD
 
     def quad_of(p, r, first):
-        return kv[p // 2, pl.ds((p % 2) * 2, 2), :, rows(r), first : first + HD].reshape(QUAD * RC, HD)
+        return kv[first, p // 2, pl.ds((p % 2) * 2, 2), :, rows(r)].reshape(QUAD * RC, HD)
 
     def unit(i, r):
         at = pl.ds(i * TILE, TILE)
@@ -291,19 +300,20 @@
 
     def values(i):
         final = mbuf[i, R - 1]
-        out = jnp.zeros((TILE, HD), jnp.float32)
-        for r in range(R):
-            factor = None if r == R - 1 else jnp.exp2(mbuf[i, r] - final)
-
-            def body(p, out):
+        for r in range(R - 1):
+            mbuf[i, r] = jnp.exp2(mbuf[i, r] - final)
+
+        def body(p, out):
+            for r in range(R):
                 e = sbuf[i, r, p]
-                if factor is not None:
-                    e = jnp.concatenate([e[:, j * RC : (j + 1) * RC] * factor for j in range(QUAD)], axis=1)
-                return out + jnp.dot(
-                    e.astype(jnp.bfloat16), quad_of(p, r, HD), preferred_element_type=jnp.float32
+                if r < R - 1:
+                    e = jnp.concatenate([e[:, j * RC : (j + 1) * RC] * mbuf[i, r] for j in range(QUAD)], axis=1)
+                out = out + jnp.dot(
+                    e.astype(jnp.bfloat16), quad_of(p, r, 1), preferred_element_type=jnp.float32
                 )
-
-            out = lax.fori_loop(0, quads + 1, body, out)
+            return out
+
+        out = lax.fori_loop(0, quads + 1, body, jnp.zeros((TILE, HD), jnp.float32))
         out = (out / jnp.sum(lbuf[i], axis=1, keepdims=True)).astype(jnp.bfloat16)
         at = pl.ds(i * (TILE // 2), TILE // 2)
         abuf[at, 0:HD] = out[: TILE // 2]
@@ -330,13 +340,15 @@
                 load_wq.wait()
             a_finish(r)
             project(r)
-            b_step(r, 0)
+            if r < R - 1:
+                b_step(r, 0)
+            else:
+                b_step(r, 0, 0)
+                b_step(r, 0, 1)
         elif what == "b":
-            b_step(int(number[0]), int(number[2]))
+            b_step(int(number[0]), int(number[2]), "kv".find(number[3:]) if number[3:] else 2)
         else:
             unit(int(number[0]), int(number[2]))
-    for i in range(2):
-        unit(i, R - 1)
 
     count = jnp.int32(0)
     index = [jnp.int32(0)] * CAP
@@ -346,13 +358,8 @@
             index[s] = jnp.where(hit & (count == s), bb, index[s])
         count = count + hit.astype(jnp.int32)
     for s in range(CAP):
-        @pl.when(t % 2 == 0)
-        def _():
-            cbuf[s] = jnp.where(s < count, kv[index[s] // 8, (index[s] // 2) % 4, index[s] % 2, :, 0:HD], jnp.zeros((TOK, HD), jnp.bfloat16))
-
-        @pl.when(t % 2 == 1)
-        def _():
-            cbuf[s] = jnp.where(s < count, kv[index[s] // 8, (index[s] // 2) % 4, index[s] % 2, :, HD:], jnp.zeros((TOK, HD), jnp.bfloat16))
+        mine = kv[t % 2, index[s] // 8, (index[s] // 2) % 4, index[s] % 2]
+        cbuf[s] = jnp.where(s < count, mine, jnp.zeros((TOK, HD), jnp.bfloat16))
     store_cache = pltpu.make_async_copy(cbuf, cache_ref, loc_sem.at[2])
     store_cache.start()
 
@@ -383,7 +390,7 @@
             pltpu.VMEM((4, 4, TOK, FD), bf16),
             pltpu.VMEM((NT, FD, 2 * HD), bf16),
             pltpu.VMEM((NT, 4, 2, PART, 2 * HD), bf16),
-            pltpu.VMEM((2, 4, 2, TOK, 2 * HD), bf16),
+            pltpu.VMEM((2, 2, 4, 2, TOK, HD), bf16),
             pltpu.VMEM((2, RC, 2 * HD), f32),
             pltpu.VMEM((2 * TILE, HD), bf16),
             pltpu.VMEM((2, R, NB // QUAD, TILE, QUAD * RC), f32),
@@ -397,9 +404,9 @@
             dma((1,)), dma((1,)),
             dma((1,)), dma((1,)),
             dma((1,)), dma((1,)),
-            dma((R, 2)), dma((1,)),
-            dma((R,)), dma((1,)),
-            dma((R,)), dma((1,)),
+            dma((R + 1, 2)), dma((1,)),
+            dma((R + 1,)), dma((1,)),
+            dma((R + 1,)), dma((1,)),
             dma((1,)),
         ],
         compiler_params=pltpu.CompilerParams(

time: 90.5 us -> 85.8 us (0.948)
  Pallas kernels: 84.9 us -> 80.2 us
    pallas_call x1, Pallas kernels: 84.9 us -> 80.2 us  [local(): pl.pallas_call(kernel, out_shape=(jax.ShapeDtypeStruct((TOK, 2 * HD), bf1...]
where the time goes in v3:
time: 85.8 us; the launch traced here: 84.8 us
  Pallas kernels  80.2 us (93%)
  local copies, waits for them, and re-layouts  3.94 us (5%)
    pallas_call x1, Pallas kernels, local(): pl.pallas_call(kernel, out_shape=(jax.ShapeDtypeStruct((TOK, 2 * HD), bf1...  80.2 us
    unnamed x2, local copies, waits for them, and re-layouts  3.94 us

profile of v3, /device:TPU:153, one launch (start us, length us, event | category | flops | bytes accessed | tf_op | source)
XLA Modules:
  0.0 84.8 jit_solution(1272184040141153614)
XLA Ops:
  0.6 80.2 %shard_map.68 = (bf16[512,256]{1,0:T(8,128)(2,1)}, bf16[8,512,128]{2,1,0:T(8,128)(2,1)}) custom-call(bf16[512,256]{1,0:T(8,128)(2,1)} %hidden_ref.1, bf16[16,256,256]{2,1,0:T(8,128)(2,1)} %bitcast.4, bf16[256,2048]{1,0:T(8,128)(2,1)} %wkv_ref.1, s32[16]{0:T(128)} %bitcast.5, s32[16]{0:T(128)} %hosts_ref.1), custom_call_target="tpu_custom_call" | custom-call | flops 8000000000 | bytes 8388608 | tf_op jit(solution)/shard_map/pallas_call | solution.py:381
  80.9 1.7 %copy.9 = bf16[512,256]{1,0:T(8,128)(2,1)} copy(bf16[512,256]{1,0:T(8,128)(2,1)} %get-tuple-element.8) | data formatting | bytes 524288
  82.6 2.3 %copy.10 = bf16[1,8,512,128]{3,2,1,0:T(8,128)(2,1)} copy(bf16[1,8,512,128]{3,2,1,0:T(8,128)(2,1)} %bitcast.3) | data formatting | bytes 2097152

commit v4 on v3

--- a/solution.py
+++ b/solution.py
@@ -34,28 +34,30 @@
 
 
 def steps():
-    at = {3: ["w0"], 8: ["w1"], 10: ["w2"], 11: ["p0"], 13: ["p1"], 15: ["b0.1"]}
+    at = {
+        0: ["wa", "wb", "wc"], 3: ["w0"], 9: ["w1"], 11: ["w2", "p0"], 13: ["p1"], 15: ["b0.1", "b0.n", "p2"],
+    }
     order = ["s0"]
     for s in range(len(XSEQ)):
         if s > 0:
             order.append(f"s{s}")
-        if s == 0:
-            order.append("w")
         if s + 1 < len(XSEQ):
             order.append(f"z{s + 1}")
         if s >= LAG:
             order.append(f"f{s - LAG}")
         order += at.get(s, [])
     order += [f"f{s}" for s in range(len(XSEQ) - LAG, len(XSEQ) - 1)]
-    order += ["p2", "b1.1", "b0.2", "b0.3", "p3", "u0.0", "b1.2", "u1.0", "b1.3", "b2.1", "u0.1", "u1.1"]
-    order += ["b2.2", "b3.1k", "b3.1v", "b2.3", "u0.2", "u1.2", "b3.2k", "b3.2v", "b3.3k", "u0.3", "u1.3", "b3.3v"]
+    order += ["b1.n", "b1.1", "b0.f", "b0.N", "b0.F", "un00", "uf00", "q3", "p3", "b2.n", "b2.1", "un01"]
+    order += ["uf01", "b1.f", "b3.nk", "b1.N", "b3.nv", "un10", "b3.1k", "b3.1v", "b1.F", "un11", "uf10", "uf11"]
+    order += ["b2.f", "b2.N", "b2.F", "un20", "un21", "b3.fk", "b3.fv", "b3.Nk", "un30", "un31", "b3.Nv", "b3.Fk"]
+    order += ["uf20", "uf21", "uf30", "uf31", "b3.Fv"]
     return order
 
 
 def kernel(
     hidden_ref, wq_ref, wkv_ref, routing_ref, hosts_ref,
     att_ref, cache_ref,
-    hid, wq, wkv, kv, acc, qbuf, sbuf, mbuf, lbuf, abuf, cbuf,
+    hid, wq, wkv, kv, acc, qbuf, sbuf, mbuf, top, lbuf, abuf, cbuf,
     loc_sem, z_recv, z_send, x_recv, xh_recv, x_send,
     w_recv, w_send, wy_recv, wy_send, ws_recv, ws_send,
     y_recv, y_send, s_recv, s_send, c_recv, c_send, a_sem,
@@ -89,6 +91,9 @@
     load_wq = pltpu.make_async_copy(wq_ref, wq, loc_sem.at[1])
     load_wq.start()
 
+    top[...] = jnp.full(top.shape, NEG, jnp.float32)
+    lbuf[...] = jnp.zeros_like(lbuf)
+
     barrier = pltpu.get_barrier_semaphore()
 
     def greet(dev):
@@ -137,23 +142,30 @@
         rcopy(ref, ref, x_send.at[0], x_recv.at[0, g], dev_xr).start()
         rcopy(ref, ref, x_send.at[1], x_recv.at[1, g], dev_xl).start()
         if s == len(XSEQ) - 1:
-            rcopy(ref, ref, x_send.at[2], xh_recv.at[r], dev_xo).start()
+            rcopy(ref, ref, x_send.at[2], xh_recv.at[xh_of(s)], dev_xo).start()
+
+    def xh_of(s):
+        r, k = XSEQ[s]
+        return r + k if r == R - 1 else r
 
     def a_forward(s):
         r, zp, g = piece_of(s)
         recv(hid.at[zp, xl, rows(r)], x_recv.at[0, g])
         ref = hid.at[zp, xl, half(r, 0)]
-        rcopy(ref, ref, x_send.at[2], xh_recv.at[r], dev_xr).start()
+        rcopy(ref, ref, x_send.at[2], xh_recv.at[xh_of(s)], dev_xr).start()
         recv(hid.at[zp, xr, rows(r)], x_recv.at[1, g])
         ref = hid.at[zp, xr, half(r, 1)]
-        rcopy(ref, ref, x_send.at[3], xh_recv.at[r], dev_xl).start()
+        rcopy(ref, ref, x_send.at[3], xh_recv.at[xh_of(s)], dev_xl).start()
 
     def a_finish(r):
         recv(hid.at[:, xo, rows(r)], xh_recv.at[r])
-        if r == R - 1:
+
+    def a_finish_last(k):
+        recv(hid.at[zk(k), xo, rows(R - 1)], xh_recv.at[R - 1 + k])
+        if k == 3:
             _, zp, g = piece_of(len(XSEQ) - 1)
-            recv(hid.at[zp, xl, rows(r)], x_recv.at[0, g])
-            recv(hid.at[zp, xr, rows(r)], x_recv.at[1, g])
+            recv(hid.at[zp, xl, rows(R - 1)], x_recv.at[0, g])
+            recv(hid.at[zp, xr, rows(R - 1)], x_recv.at[1, g])
 
     def a_drain():
         for kind in range(2):
@@ -171,7 +183,7 @@
             def _():
                 sent(hid.at[zp, x], z_send.at[1, zp])
 
-    def w_start():
+    def w_start(part_of):
         src_rows = pl.ds(part * PART, PART)
 
         def piece(to):
@@ -182,8 +194,9 @@
             rcopy(piece(to), wkv.at[t, y, c], w_send.at[0], w_recv.at[0], (b, to)).start()
             return carry
 
-        pltpu.make_async_copy(piece(t), wkv.at[t, y, c], w_recv.at[0]).start()
-        lax.fori_loop(1, NT, one, 0)
+        if part_of == 0:
+            pltpu.make_async_copy(piece(t), wkv.at[t, y, c], w_recv.at[0]).start()
+        lax.fori_loop(1 + 5 * part_of, 6 + 5 * part_of, one, 0)
 
     def w_step(i):
         if i == 0:
@@ -203,25 +216,44 @@
         sent(wkv.at[:, pl.ds(0, 3), c], wy_send.at[0])
         sent(wkv.at[:, :, c], ws_send.at[0])
 
+    def product(r, zp, side):
+        total = None
+        for xp in range(4):
+            rhs = wq[zp * 4 + xp] if side == 0 else wkv[zp * 4 + xp].reshape(FD, 2 * HD)
+            one = jnp.dot(hid[zp, xp, rows(r)], rhs, preferred_element_type=jnp.float32)
+            total = one if total is None else total + one
+        return total
+
+    def keep_keyval(r, total):
+        for j in range(2):
+            kv[j, h, y, c, rows(r)] = total[:, j * HD : (j + 1) * HD].astype(jnp.bfloat16)
+
+    def keep_query(r, total):
+        for head in range(2):
+            at = (r // 2) * TILE + head * (TILE // 2) + (r % 2) * RC
+            qbuf[pl.ds(at, RC)] = total[:, head * HD : (head + 1) * HD].astype(jnp.bfloat16)
+
     def project(r):
         acc[...] = jnp.zeros_like(acc)
 
         def body(zp, carry):
             for side in range(2):
-                total = None
-                for xp in range(4):
-                    rhs = wq[zp * 4 + xp] if side == 0 else wkv[zp * 4 + xp].reshape(FD, 2 * HD)
-                    one = jnp.dot(hid[zp, xp, rows(r)], rhs, preferred_element_type=jnp.float32)
-                    total = one if total is None else total + one
-                acc[side] += total
+                acc[side] += product(r, zp, side)
             return carry
 
         lax.fori_loop(0, 4, body, 0)
-        for j in range(2):
-            kv[j, h, y, c, rows(r)] = acc[1, :, j * HD : (j + 1) * HD].astype(jnp.bfloat16)
-        for head in range(2):
-            at = (r // 2) * TILE + head * (TILE // 2) + (r % 2) * RC
-            qbuf[pl.ds(at, RC)] = acc[0, :, head * HD : (head + 1) * HD].astype(jnp.bfloat16)
+        keep_keyval(r, acc[1])
+        keep_query(r, acc[0])
+
+    def project_last(part):
+        r = R - 1
+        if part == 0:
+            for side in range(2):
+                acc[side] = product(r, zk(0), side) + product(r, zk(1), side)
+        elif part == 1:
+            keep_keyval(r, acc[1] + product(r, zk(2), 1) + product(r, zk(3), 1))
+        else:
+            keep_query(r, acc[0] + product(r, zk(2), 0) + product(r, zk(3), 0))
 
     def sides(part):
         return pl.ds(0, 2) if part == 2 else pl.ds(part, 1)
@@ -238,22 +270,22 @@
         hh = (h + far) % 2
         recv(kv.at[sides(part), hh, pl.ds(0, 3), c, rows(r)], y_recv.at[slot(r, part), far])
         ref = kv.at[sides(part), hh, :, c, rows(r)]
-        rcopy(ref, ref, s_send.at[0], s_recv.at[slot(r, part)], dev_sib).start()
-
-    def b_step(r, i, part=2):
+        rcopy(ref, ref, s_send.at[0], s_recv.at[slot(r, part), far], dev_sib).start()
+
+    def b_step(r, what, part=2):
         at = slot(r, part)
-        if i == 0:
+        if what == "0":
             ref = kv.at[sides(part), h, y, c, rows(r)]
             rcopy(ref, ref, c_send.at[0], c_recv.at[at], dev_far).start()
             b_send(r, part, 0)
-        elif i == 1:
+        elif what == "1":
             recv(kv.at[sides(part), 1 - h, y, c, rows(r)], c_recv.at[at])
             b_send(r, part, 1)
-            b_share(r, part, 0)
-        elif i == 2:
-            b_share(r, part, 1)
-        else:
-            recv(kv.at[sides(part), :, :, 1 - c, rows(r)], s_recv.at[at])
+        elif what in "nf":
+            b_share(r, part, "nf".index(what))
+        else:
+            far = "NF".index(what)
+            recv(kv.at[sides(part), (h + far) % 2, :, 1 - c, rows(r)], s_recv.at[at, far])
 
     def b_drain():
         sent(kv.at[:, 0, pl.ds(0, 3)], y_send.at[0])
@@ -265,49 +297,52 @@
     def quad_of(p, r, first):
         return kv[first, p // 2, pl.ds((p % 2) * 2, 2), :, rows(r)].reshape(QUAD * RC, HD)
 
-    def unit(i, r):
-        at = pl.ds(i * TILE, TILE)
-        q = qbuf[at]
-        start = jnp.full((TILE, HD), NEG, jnp.float32) if r == 0 else mbuf[i, r - 1]
+    def unit(i, r, far):
+        q = qbuf[pl.ds(i * TILE, TILE)]
 
         def scores(p):
             return SCALE2 * lax.dot_general(
                 q, quad_of(p, r, 0), (((1,), (1,)), ((), ())), preferred_element_type=jnp.float32
             )
 
-        def keep(p, s, m):
-            sbuf[i, r, p] = s
-            for j in range(QUAD):
-                m = jnp.maximum(m, s[:, j * RC : (j + 1) * RC])
-            return m
-
-        m = lax.fori_loop(0, quads, lambda p, m: keep(p, scores(p), m), start)
-        row = lax.broadcasted_iota(jnp.int32, (TILE, QUAD * RC), 0) % (TILE // 2) + (b * TOK + i * (TILE // 2))
-        col = lax.broadcasted_iota(jnp.int32, (TILE, QUAD * RC), 1)
-        col = col % RC + (col // RC) * TOK + (quads * QUAD * TOK + r * RC)
-        m = keep(quads, jnp.where(col <= row, scores(quads), NEG), m)
-        m = jnp.broadcast_to(jnp.max(m, axis=1, keepdims=True), (TILE, HD))
-        mbuf[i, r] = m
-
-        def exps(p, total):
-            s = sbuf[i, r, p]
-            e = [jnp.exp2(s[:, j * RC : (j + 1) * RC] - m) for j in range(QUAD)]
+        def keep(p, s):
+            s = [s[:, j * RC : (j + 1) * RC] for j in range(QUAD)]
+            m = jnp.maximum(jnp.maximum(s[0], s[1]), jnp.maximum(s[2], s[3]))
+            m = jnp.broadcast_to(jnp.max(m, axis=1, keepdims=True), (TILE, HD))
+            mbuf[i, r, p] = m
+            e = [jnp.exp2(one - m) for one in s]
             sbuf[i, r, p] = jnp.concatenate(e, axis=1)
-            return total + ((e[0] + e[1]) + (e[2] + e[3]))
-
-        total = jnp.zeros((TILE, HD), jnp.float32) if r == 0 else lbuf[i] * jnp.exp2(start - m)
-        lbuf[i] = lax.fori_loop(0, quads + 1, exps, total)
+            old = top[i]
+            new = jnp.maximum(old, m)
+            lbuf[i] = lbuf[i] * jnp.exp2(old - new) + ((e[0] + e[1]) + (e[2] + e[3])) * jnp.exp2(m - new)
+            top[i] = new
+
+        def whole(p, carry):
+            keep(p, scores(p))
+            return carry
+
+        if far:
+            lax.fori_loop(0, 2, whole, 0)
+        else:
+            lax.fori_loop(2 * h, quads, whole, 0)
+            row = lax.broadcasted_iota(jnp.int32, (TILE, QUAD * RC), 0) % (TILE // 2) + (b * TOK + i * (TILE // 2))
+            col = lax.broadcasted_iota(jnp.int32, (TILE, QUAD * RC), 1)
+            col = col % RC + (col // RC) * TOK + (quads * QUAD * TOK + r * RC)
+            keep(quads, jnp.where(col <= row, scores(quads), NEG))
+
+    def unit_if_any(i, r, far):
+        if far:
+            pl.when(h == 1)(lambda: unit(i, r, far))
+        else:
+            unit(i, r, far)
 
     def values(i):
-        final = mbuf[i, R - 1]
-        for r in range(R - 1):
-            mbuf[i, r] = jnp.exp2(mbuf[i, r] - final)
+        final = top[i]
 
         def body(p, out):
             for r in range(R):
-                e = sbuf[i, r, p]
-                if r < R - 1:
-                    e = jnp.concatenate([e[:, j * RC : (j + 1) * RC] * mbuf[i, r] for j in range(QUAD)], axis=1)
+                e, f = sbuf[i, r, p], jnp.exp2(mbuf[i, r, p] - final)
+                e = jnp.concatenate([e[:, j * RC : (j + 1) * RC] * f for j in range(QUAD)], axis=1)
                 out = out + jnp.dot(
                     e.astype(jnp.bfloat16), quad_of(p, r, 1), preferred_element_type=jnp.float32
                 )
@@ -333,22 +368,28 @@
         elif what == "f":
             a_forward(int(number))
         elif what == "w":
-            w_step(int(number)) if number else w_start()
+            w_start("abc".index(number)) if number in "abc" else w_step(int(number))
+        elif what == "q":
+            for k in range(2):
+                a_finish_last(k)
+            project_last(0)
+        elif what == "p" and int(number) == R - 1:
+            for k in range(2, 4):
+                a_finish_last(k)
+            project_last(1)
+            b_step(R - 1, "0", 0)
+            b_step(R - 1, "0", 1)
+            project_last(2)
         elif what == "p":
-            r = int(number)
-            if r == 0:
+            if number == "0":
                 load_wq.wait()
-            a_finish(r)
-            project(r)
-            if r < R - 1:
-                b_step(r, 0)
-            else:
-                b_step(r, 0, 0)
-                b_step(r, 0, 1)
+            a_finish(int(number))
+            project(int(number))
+            b_step(int(number), "0")
         elif what == "b":
-            b_step(int(number[0]), int(number[2]), "kv".find(number[3:]) if number[3:] else 2)
-        else:
-            unit(int(number[0]), int(number[2]))
+            b_step(int(number[0]), number[2], "kv".index(number[3]) if number[3:] else 2)
+        else:
+            unit_if_any(int(number[2]), int(number[1]), "nf".index(number[0]))
 
     count = jnp.int32(0)
     index = [jnp.int32(0)] * CAP
@@ -371,6 +412,20 @@
     b_drain()
     store_cache.wait()
     pltpu.make_async_copy(abuf, att_ref, a_sem.at[0]).wait()
+
+
+def hand_on(att_in, cache_in, att_out, cache_out, att, cache, sem_in, sem_out):
+    parts = [(att_in, att, att_out, pl.ds(0, TOK))]
+    parts += [(cache_in, cache, cache_out, pl.ds(2 * i, 2)) for i in range(CAP // 2)]
+    loads = [pltpu.make_async_copy(a.at[at], v.at[at], sem_in.at[i]) for i, (a, v, _, at) in enumerate(parts)]
+    stores = [pltpu.make_async_copy(v.at[at], o.at[at], sem_out.at[i]) for i, (_, v, o, at) in enumerate(parts)]
+    for load in loads:
+        load.start()
+    for load, store in zip(loads, stores):
+        load.wait()
+        store.start()
+    for store in stores:
+        store.wait()
 
 
 def local(hidden_in, w_query, w_keyval, routing, hosts):
@@ -394,26 +449,40 @@
             pltpu.VMEM((2, RC, 2 * HD), f32),
             pltpu.VMEM((2 * TILE, HD), bf16),
             pltpu.VMEM((2, R, NB // QUAD, TILE, QUAD * RC), f32),
-            pltpu.VMEM((2, R, TILE, HD), f32),
+            pltpu.VMEM((2, R, NB // QUAD, TILE, HD), f32),
+            pltpu.VMEM((2, TILE, HD), f32),
             pltpu.VMEM((2, TILE, HD), f32),
             pltpu.VMEM((TOK, 2 * HD), bf16),
             pltpu.VMEM((CAP, TOK, HD), bf16),
             dma((3,)),
             dma((4 * R,)), dma((2, 4)),
-            dma((2, 4 * R)), dma((R,)), dma((4,)),
+            dma((2, 4 * R)), dma((R + 3,)), dma((4,)),
             dma((1,)), dma((1,)),
             dma((1,)), dma((1,)),
             dma((1,)), dma((1,)),
             dma((R + 1, 2)), dma((1,)),
-            dma((R + 1,)), dma((1,)),
+            dma((R + 1, 2)), dma((1,)),
             dma((R + 1,)), dma((1,)),
             dma((1,)),
         ],
         compiler_params=pltpu.CompilerParams(
-            collective_id=0, has_side_effects=True, vmem_limit_bytes=58 * 1024 * 1024
+            collective_id=0, has_side_effects=True, vmem_limit_bytes=60 * 1024 * 1024
         ),
         cost_estimate=pl.CostEstimate(flops=8 * 10**9, bytes_accessed=8 * 2**20, transcendentals=8 * 2**20),
     )(hidden_in, w_query.reshape(NT, FD, 2 * HD), w_keyval, routing.reshape(NB), hosts)
+    attended, cache = pl.pallas_call(
+        hand_on,
+        out_shape=(
+            jax.ShapeDtypeStruct((TOK, 2 * HD), bf16),
+            jax.ShapeDtypeStruct((CAP, TOK, HD), bf16),
+        ),
+        in_specs=[any_spec, any_spec],
+        out_specs=(any_spec, any_spec),
+        scratch_shapes=[
+            pltpu.VMEM((TOK, 2 * HD), bf16), pltpu.VMEM((CAP, TOK, HD), bf16),
+            dma((1 + CAP // 2,)), dma((1 + CAP // 2,)),
+        ],
+    )(attended, cache)
     return attended, cache[None]
 
 

time: 85.8 us -> 83.5 us (0.973)
  local copies, waits for them, and re-layouts: 3.94 us -> 0 us
  Pallas kernels: 80.2 us -> 82.1 us
    unnamed x2 -> x0, local copies, waits for them, and re-layouts: 3.94 us -> none
    pallas_call x0 -> x1, Pallas kernels: none -> 2.08 us  [local(): pl.pallas_call(hand_on, out_shape=(jax.ShapeDtypeStruct((TOK, 2 * HD), bf...]
where the time goes in v4:
time: 83.5 us; the launch traced here: 82.9 us
  Pallas kernels  82.1 us (98%)
    pallas_call x1, Pallas kernels, local(): pl.pallas_call(kernel, out_shape=(jax.ShapeDtypeStruct((TOK, 2 * HD), bf1...  80 us
    pallas_call x1, Pallas kernels, local(): pl.pallas_call(hand_on, out_shape=(jax.ShapeDtypeStruct((TOK, 2 * HD), bf...  2.08 us

profile of v4, /device:TPU:153, one launch (start us, length us, event | category | flops | bytes accessed | tf_op | source)
XLA Modules:
  0.0 82.9 jit_solution(2576079081084002820)
XLA Ops:
  0.6 80.0 %shard_map.68 = (bf16[512,256]{1,0:T(8,128)(2,1)}, bf16[8,512,128]{2,1,0:T(8,128)(2,1)}) custom-call(bf16[512,256]{1,0:T(8,128)(2,1)} %hidden_ref.1, bf16[16,256,256]{2,1,0:T(8,128)(2,1)} %bitcast.3, bf16[256,2048]{1,0:T(8,128)(2,1)} %wkv_ref.1, s32[16]{0:T(128)} %bitcast.5, s32[16]{0:T(128)} %hosts_ref.1), custom_call_target="tpu_custom_call" | custom-call | flops 8000000000 | bytes 8388608 | tf_op jit(solution)/shard_map/pallas_call | solution.py:436
  80.7 2.1 %shard_map.69 = (bf16[512,256]{1,0:T(8,128)(2,1)}, bf16[8,512,128]{2,1,0:T(8,128)(2,1)}) custom-call(bf16[512,256]{1,0:T(8,128)(2,1)} %get-tuple-element.6.att_in, bf16[8,512,128]{2,1,0:T(8,128)(2,1)} %get-tuple-element.7.cache_in), custom_call_target="tpu_custom_call" | custom-call | tf_op jit(solution)/shard_map/pallas_call | solution.py:473

commit v5 on v4

--- a/solution.py
+++ b/solution.py
@@ -35,7 +35,7 @@
 
 def steps():
     at = {
-        0: ["wa", "wb", "wc"], 3: ["w0"], 9: ["w1"], 11: ["w2", "p0"], 13: ["p1"], 15: ["b0.1", "b0.n", "p2"],
+        0: ["wa", "wb", "wc"], 3: ["w0"], 9: ["w1"], 11: ["w2", "p0"], 13: ["p1"], 15: ["b0.1", "b0.n"],
     }
     order = ["s0"]
     for s in range(len(XSEQ)):
@@ -47,10 +47,10 @@
             order.append(f"f{s - LAG}")
         order += at.get(s, [])
     order += [f"f{s}" for s in range(len(XSEQ) - LAG, len(XSEQ) - 1)]
-    order += ["b1.n", "b1.1", "b0.f", "b0.N", "b0.F", "un00", "uf00", "q3", "p3", "b2.n", "b2.1", "un01"]
-    order += ["uf01", "b1.f", "b3.nk", "b1.N", "b3.nv", "un10", "b3.1k", "b3.1v", "b1.F", "un11", "uf10", "uf11"]
-    order += ["b2.f", "b2.N", "b2.F", "un20", "un21", "b3.fk", "b3.fv", "b3.Nk", "un30", "un31", "b3.Nv", "b3.Fk"]
-    order += ["uf20", "uf21", "uf30", "uf31", "b3.Fv"]
+    order += ["b1.n", "b0.N", "un00", "p2", "b1.1", "b0.f", "b1.N", "un10", "b0.F", "uf00", "q3", "p3"]
+    order += ["b2.n", "b2.1", "un01", "uf01", "b1.f", "b3.nk", "b3.nv", "un11", "b3.1k", "b3.1v", "b1.F", "uf10"]
+    order += ["uf11", "b2.f", "b2.N", "b2.F", "un20", "un21", "b3.fk", "b3.fv", "b3.Nk", "un30", "un31", "b3.Nv"]
+    order += ["b3.Fk", "uf20", "uf21", "uf30", "uf31", "b3.Fv"]
     return order
 
 

time: 83.5 us -> 81.8 us (0.980)
  Pallas kernels: 82.1 us -> 80.8 us
    pallas_call x1, Pallas kernels: 80 us -> 78.7 us  [local(): pl.pallas_call(kernel, out_shape=(jax.ShapeDtypeStruct((TOK, 2 * HD), bf1...]
where the time goes in v5:
time: 81.8 us; the launch traced here: 81.6 us
  Pallas kernels  80.8 us (99%)
    pallas_call x1, Pallas kernels, local(): pl.pallas_call(kernel, out_shape=(jax.ShapeDtypeStruct((TOK, 2 * HD), bf1...  78.7 us
    pallas_call x1, Pallas kernels, local(): pl.pallas_call(hand_on, out_shape=(jax.ShapeDtypeStruct((TOK, 2 * HD), bf...  2.08 us

profile of v5, /device:TPU:153, one launch (start us, length us, event | category | flops | bytes accessed | tf_op | source)
XLA Modules:
  0.0 81.6 jit_solution(11170432555656808238)
XLA Ops:
  0.6 78.7 %shard_map.68 = (bf16[512,256]{1,0:T(8,128)(2,1)}, bf16[8,512,128]{2,1,0:T(8,128)(2,1)}) custom-call(bf16[512,256]{1,0:T(8,128)(2,1)} %hidden_ref.1, bf16[16,256,256]{2,1,0:T(8,128)(2,1)} %bitcast.3, bf16[256,2048]{1,0:T(8,128)(2,1)} %wkv_ref.1, s32[16]{0:T(128)} %bitcast.5, s32[16]{0:T(128)} %hosts_ref.1), custom_call_target="tpu_custom_call" | custom-call | flops 8000000000 | bytes 8388608 | tf_op jit(solution)/shard_map/pallas_call | solution.py:436
  79.3 2.1 %shard_map.69 = (bf16[512,256]{1,0:T(8,128)(2,1)}, bf16[8,512,128]{2,1,0:T(8,128)(2,1)}) custom-call(bf16[512,256]{1,0:T(8,128)(2,1)} %get-tuple-element.6.att_in, bf16[8,512,128]{2,1,0:T(8,128)(2,1)} %get-tuple-element.7.cache_in), custom_call_target="tpu_custom_call" | custom-call | tf_op jit(solution)/shard_map/pallas_call | solution.py:473
